TPU v7x, 512 devices: a whole 4x4x16 slice. The times are simulated.
512 devices in a mesh: dp: 4 (over x), expert: 128 (over y, z, core).
Axes of the slice: x: 4, y: 4, z: 16, core: 2. Of those that a mesh axis runs over, the one named last changes fastest.
Arguments:
- grads: bfloat16 [65536, 1024], P(('dp', 'expert')), may hold values from -6 to 6
- route_weight: float32 [65536, 8], P(('dp', 'expert')), may hold values from 0.1 to 1
- routes: int32 [65536, 8], P(('dp', 'expert')), may hold values from 0 to 127, all different within a row; in each aligned block of 128 rows (0 to 127, 128 to 255, ...) at most 12 rows name the same one
- hot: int32 [128], replicated, may hold values from 0 to 1, as said below
- expert_inputs: bfloat16 [4, 128, 128, 1, 2, 4, 768], P('dp', 'expert'), may hold values from -6 to 6
Outputs:
- input_factor: float32 [768, 128, 768], P('dp', 'expert')
- grad_factor: float32 [1024, 128, 1024], P('dp', 'expert')
Inputs may be any that keep to these rules, and one draw needn't show every extreme that they name: `routes`: within each device's 128 tokens no expert is chosen more than 3 * 4 times, and some expert exactly that often. Every expert e with e >= 64 has hot[e] = 1; the others have a replica or not.
All inputs are finite; a program needn't handle non-finite values.
Results may differ from a plain program's by a relative error of at most 0.013.
Values may be sent and summed in bfloat16 or wider, within the bound.
A program may use at most 64 MiB of HBM per device.

v0:
```python
import jax
import jax.numpy as jnp
from jax import lax
from jax.sharding import PartitionSpec as P


def partner(block, axis, distance):
    count = lax.axis_size(axis)
    route = []
    for low in range(count):
        high = low | 1 << distance
        if high != low and high < count:
            route += [(low, high), (high, low)]
    return lax.ppermute(block, axis, route)


def gram_rows(left, right):
    return jnp.einsum("nlcf,nlcg->flg", left, right, preferred_element_type=jnp.float32)


def shards(grads, route_weight, routes, hot, expert_inputs):
    n_exp = lax.axis_size("expert")
    n_data = lax.axis_size("dp")
    tok_dev = grads.shape[0]
    width = grads.shape[1]
    top = routes.shape[1]
    experts = hot.shape[0]
    exp_dev = experts // n_exp
    cap = expert_inputs.shape[5]
    hidden = expert_inputs.shape[6]
    half = n_exp // 2
    labels = jnp.arange(experts, dtype=jnp.int32)
    onehot = (routes[:, :, None] == labels[None, None, :]).astype(jnp.float32)
    counts = jnp.sum(onehot, axis=1)
    lower = (jnp.arange(tok_dev)[:, None] > jnp.arange(tok_dev)[None, :]).astype(jnp.float32)
    before = jnp.dot(lower, counts, precision=lax.Precision.HIGHEST)
    rank = jnp.sum(onehot * before[:, None, :], axis=2).astype(jnp.int32)
    hot_pick = jnp.sum(onehot * hot.astype(jnp.float32)[None, None, :], axis=2) > 0.5
    own = rank < cap
    spill = (rank >= cap) & (rank < 2 * cap) & hot_pick
    owner = routes // exp_dev
    local = routes % exp_dev
    dest = jnp.where(own, owner, jnp.bitwise_xor(owner, half))
    part = jnp.where(own, 0, 1)
    slot = jnp.where(own, rank, rank - cap)
    total = n_exp * exp_dev * 2 * cap
    index = jnp.where(
        own | spill, ((dest * exp_dev + local) * 2 + part) * cap + slot, total
    ).reshape(-1)
    scaled = (route_weight[:, :, None] * grads[:, None, :].astype(jnp.float32)).astype(jnp.bfloat16)
    send_rows = (
        jnp.zeros((total, width), jnp.bfloat16)
        .at[index]
        .set(scaled.reshape(-1, width), mode="drop")
    )
    send_occ = (
        jnp.zeros((total,), jnp.bfloat16)
        .at[index]
        .set(jnp.ones(index.shape, jnp.bfloat16), mode="drop")
    )
    recv_rows, recv_occ = (
        lax.all_to_all(
            send_rows.reshape(n_exp, exp_dev, 2, cap, width),
            "expert",
            split_axis=0,
            concat_axis=0,
            tiled=True,
        ),
        lax.all_to_all(
            send_occ.reshape(n_exp, exp_dev, 2, cap),
            "expert",
            split_axis=0,
            concat_axis=0,
            tiled=True,
        ),
    )
    inputs = expert_inputs.reshape(n_exp, exp_dev, 2, cap, hidden) * recv_occ[..., None]
    own_in = inputs[:, :, 0]
    own_grad = recv_rows[:, :, 0]
    rep_in = inputs[:, :, 1]
    rep_grad = recv_rows[:, :, 1]
    bit = n_exp.bit_length() - 2
    rep_a = jnp.einsum("nlcf,nlcg->flg", rep_in, rep_in, preferred_element_type=jnp.float32).astype(
        jnp.bfloat16
    )
    rep_g = jnp.einsum(
        "nlcf,nlcg->flg", rep_grad, rep_grad, preferred_element_type=jnp.float32
    ).astype(jnp.bfloat16)
    far_a, far_g = partner((rep_a, rep_g), "expert", bit)
    far_a = far_a.astype(jnp.float32)
    far_g = far_g.astype(jnp.float32)
    input_share = lax.psum_scatter(
        (gram_rows(own_in, own_in) + far_a).astype(jnp.bfloat16),
        "dp",
        scatter_dimension=0,
        tiled=True,
    ).astype(jnp.float32)
    grad_share = lax.psum_scatter(
        (gram_rows(own_grad, own_grad) + far_g).astype(jnp.bfloat16),
        "dp",
        scatter_dimension=0,
        tiled=True,
    ).astype(jnp.float32)
    factor = 1.0 / (top * tok_dev * n_data)
    return (input_share * factor, grad_share * factor)


def solution(mesh):
    return jax.shard_map(
        shards,
        mesh=mesh,
        in_specs=(
            P(("dp", "expert"), None),
            P(("dp", "expert"), None),
            P(("dp", "expert"), None),
            P(),
            P("dp", "expert", None, None, None, None, None),
        ),
        out_specs=(P("dp", "expert", None), P("dp", "expert", None)),
        check_vma=False,
    )
```

profile of v0, /device:TPU:1, one launch (start us, length us, event | category | flops | bytes accessed | tf_op | source)
XLA Modules:
  0.0 264.2 jit_solution(5023288285133580253)
XLA Ops:
  7.2 0.8 copy.43
  8.0 0.2 convert_reduce_fusion
  8.2 0.2 fusion.16
  8.4 0.7 convert_element_type.56
  9.0 0.5 select_reduce_fusion
  9.6 0.1 reshape.100
  9.7 7.6 %scatter_custom_fusion = bf16[1024]{0:T(1024)(128)(2,1)S(1)} fusion(s32[1024]{0:T(1024)S(1)} %bitcast.63, bf16[1024]{0:T(1024)(128)(2,1)S(1)} %broadcast.70, bf16[]{:T(256)} %constant.21.clone.1), kind=kCustom, calls=%fused_computation.43 | custom fusion | bytes 2050 | tf_op jit(solution)/shard_map/scatter | solution.py:59
  17.3 0.8 reshape.101
  18.1 20.6 %all-to-all-start = ((bf16[128,1,2,4]{3,2,1,0:T(2,128)(2,1)}), bf16[128,1,2,4]{3,2,1,0:T(2,128)(2,1)S(1)}, u32[]{:S(2)}, u32[]{:S(2)}) async-start(bf16[128,1,2,4]{3,2,1,0:T(2,128)(2,1)} %bitcast.2), calls=%async_computation | async-start | bytes 131072 | tf_op jit(solution)/shard_map/all_to_all | solution.py:69
  38.6 1.0 convert_element_type.63
  39.6 0.8 copy.50
  40.4 0.1 mul.85
  40.5 6.3 %scatter_custom_fusion.1 = bf16[1024,1024]{1,0:T(8,128)(2,1)S(1)} fusion(s32[1024]{0:T(1024)S(1)} %bitcast.64, f32[128,1024]{1,0:T(8,128)S(1)} %convert_element_type.63, f32[1024]{0:T(1024)S(1)} %mul.85, bf16[]{:T(256)} %constant.21.clone.1), kind=kCustom, calls=%fused_computation.10 | custom fusion | flops 2097152 | bytes 2625538 | tf_op jit(solution)/shard_map/scatter | solution.py:54
  46.8 2.2 reshape.104
  49.1 4.5 %all-to-all-done = bf16[128,1,2,4]{3,2,1,0:T(2,128)(2,1)S(1)} async-done(((bf16[128,1,2,4]{3,2,1,0:T(2,128)(2,1)}), bf16[128,1,2,4]{3,2,1,0:T(2,128)(2,1)S(1)}, u32[]{:S(2)}, u32[]{:S(2)}) %all-to-all-start) | async-done | bytes 2080 | tf_op jit(solution)/shard_map/all_to_all | solution.py:69
  53.6 11.7 %all-to-all-start.1 = ((bf16[128,1,2,4,1024]{4,3,2,1,0:T(4,128)(2,1)}), bf16[128,1,2,4,1024]{4,3,2,1,0:T(4,128)(2,1)S(1)}, u32[]{:S(2)}, u32[]{:S(2)}) async-start(bf16[128,1,2,4,1024]{4,3,2,1,0:T(4,128)(2,1)} %bitcast.61), calls=%async_computation.1 | async-start | bytes 4194304 | tf_op jit(solution)/shard_map/all_to_all | solution.py:62
  65.3 0.0 reduce-scatter.7.cloned.1.call-start
  65.3 0.1 copy.47
  65.4 2.0 bitcast_multiply_fusion.1
  67.4 0.0 copy-start
  67.4 1.8 fusion.8
  69.2 0.0 copy-done
  69.2 5.1 %collective-permute-start = (bf16[768,1,768]{0,2,1:T(8,128)(2,1)}, bf16[768,1,768]{0,2,1:T(8,128)(2,1)}, u32[]{:S(2)}, u32[]{:S(2)}) collective-permute-start(bf16[768,1,768]{0,2,1:T(8,128)(2,1)} %fusion.8), channel_id=1, source_target_pairs={{0,64},{64,0},{1,65},{65,1},{2,66},{66,2},{3,67},{67,3},{4,68},{68... | collective-permute-start | bytes 3538952 | tf_op jit(solution)/shard_map/ppermute | solution.py:14
  74.3 90.1 %all-to-all-done.1 = bf16[128,1,2,4,1024]{4,3,2,1,0:T(4,128)(2,1)S(1)} async-done(((bf16[128,1,2,4,1024]{4,3,2,1,0:T(4,128)(2,1)}), bf16[128,1,2,4,1024]{4,3,2,1,0:T(4,128)(2,1)S(1)}, u32[]{:S(2)}, u32[]{:S(2)}) %all-to-all-start.1) | async-done | bytes 2097184 | tf_op jit(solution)/shard_map/all_to_all | solution.py:62
  164.4 0.7 fusion.21
  165.1 0.0 copy-start.1
  165.1 2.8 %fusion.7 = bf16[1024,1,1024]{0,2,1:T(8,128)(2,1)} fusion(bf16[128,1,1,4,1024]{4,3,2,1,0:T(4,128)(2,1)S(1)} %get-tuple-element.13), kind=kOutput, calls=%fused_computation.13 | convolution fusion | flops 1074790400 | bytes 3145728 | tf_op jit(solution)/shard_map/nlcf,nlcg->flg/dot_general | solution.py:86
  168.0 4.7 %collective-permute-start.1 = (bf16[1024,1,1024]{0,2,1:T(8,128)(2,1)}, bf16[1024,1,1024]{0,2,1:T(8,128)(2,1)}, u32[]{:S(2)}, u32[]{:S(2)}) collective-permute-start(bf16[1024,1,1024]{0,2,1:T(8,128)(2,1)} %fusion.7), channel_id=1, source_target_pairs={{0,64},{64,0},{1,65},{65,1},{2,66},{66,2},{3,67},{67,3},{4,68},{68... | collective-permute-start | bytes 6291464 | tf_op jit(solution)/shard_map/ppermute | solution.py:14
  172.7 0.0 collective-permute-done
  172.7 0.0 copy-done.1
  172.7 2.1 fusion.9
  174.8 1.5 copy.64
  176.3 0.0 reduce-scatter.7.cloned.1.call-update
  176.3 0.0 reduce-scatter.5.cloned.1.call-start
  176.3 41.9 %collective-permute-done.1 = bf16[1024,1,1024]{0,2,1:T(8,128)(2,1)} collective-permute-done((bf16[1024,1,1024]{0,2,1:T(8,128)(2,1)}, bf16[1024,1,1024]{0,2,1:T(8,128)(2,1)}, u32[]{:S(2)}, u32[]{:S(2)}) %collective-permute-start.1) | collective-permute-done | bytes 2097184 | tf_op jit(solution)/shard_map/ppermute | solution.py:14
  218.3 4.4 %fusion = bf16[1024,1,1024]{0,2,1:T(8,128)(2,1)} fusion(bf16[1024,1,1024]{0,2,1:T(8,128)(2,1)} %collective-permute-done.1, bf16[128,1,1,4,1024]{4,3,2,1,0:T(4,128)(2,1)S(1)} %get-tuple-element.12), kind=kOutput, calls=%fused_computation.3 | convolution fusion | flops 1076887552 | bytes 5242880 | tf_op jit(solution)/shard_map/nlcf,nlcg->flg/dot_general | solution.py:18
  222.7 0.0 reduce-scatter.5.cloned.1.call-update
  222.7 0.0 reduce-scatter.7.cloned.1.call-done
  222.7 1.1 copy.65
  223.9 0.1 convert_multiply_fusion.1
  223.9 1.1 copy.56
  225.0 29.3 %reduce-scatter.5.cloned.1.call-done = bf16[256,1,1024]{0,2,1:T(8,128)(2,1)} async-done(((bf16[1024,1,1024]{0,2,1:T(8,128)(2,1)}), bf16[256,1,1024]{0,2,1:T(8,128)(2,1)}) %reduce-scatter.5.cloned.1.call-update) | async-done | bytes 524304 | tf_op jit(solution)/shard_map/reduce_scatter | solution.py:98
  254.3 1.1 convert_multiply_fusion
  255.4 1.9 copy.57
  (3 shorter events, 0.1 us)
Async XLA Ops:
  18.1 35.5 %all-to-all-start = ((bf16[128,1,2,4]{3,2,1,0:T(2,128)(2,1)}), bf16[128,1,2,4]{3,2,1,0:T(2,128)(2,1)S(1)}, u32[]{:S(2)}, u32[]{:S(2)}) async-start(bf16[128,1,2,4]{3,2,1,0:T(2,128)(2,1)} %bitcast.2), calls=%async_computation | async-start | bytes 131072 | tf_op jit(solution)/shard_map/all_to_all | solution.py:69
  53.6 110.8 %all-to-all-start.1 = ((bf16[128,1,2,4,1024]{4,3,2,1,0:T(4,128)(2,1)}), bf16[128,1,2,4,1024]{4,3,2,1,0:T(4,128)(2,1)S(1)}, u32[]{:S(2)}, u32[]{:S(2)}) async-start(bf16[128,1,2,4,1024]{4,3,2,1,0:T(4,128)(2,1)} %bitcast.61), calls=%async_computation.1 | async-start | bytes 4194304 | tf_op jit(solution)/shard_map/all_to_all | solution.py:62
  65.3 157.5 %reduce-scatter.7.cloned.1.call-start = ((), (), s32[]{:S(2)}) async-start(), calls=%async_computation.5 | async-start | bytes 1474560
  67.4 1.8 copy-start
  69.2 103.5 %collective-permute-start = (bf16[768,1,768]{0,2,1:T(8,128)(2,1)}, bf16[768,1,768]{0,2,1:T(8,128)(2,1)}, u32[]{:S(2)}, u32[]{:S(2)}) collective-permute-start(bf16[768,1,768]{0,2,1:T(8,128)(2,1)} %fusion.8), channel_id=1, source_target_pairs={{0,64},{64,0},{1,65},{65,1},{2,66},{66,2},{3,67},{67,3},{4,68},{68... | collective-permute-start | bytes 3538952 | tf_op jit(solution)/shard_map/ppermute | solution.py:14
  165.1 7.6 %copy-start.1 = (bf16[128,1,2,4,768]{4,0,3,2,1:T(8,128)(2,1)S(1)}, bf16[128,1,2,4,768]{4,0,3,2,1:T(8,128)(2,1)}, u32[]{:S(2)}) copy-start(bf16[128,1,2,4,768]{4,0,3,2,1:T(8,128)(2,1)} %copy-done) | copy-start | bytes 4718596
  168.0 50.3 %collective-permute-start.1 = (bf16[1024,1,1024]{0,2,1:T(8,128)(2,1)}, bf16[1024,1,1024]{0,2,1:T(8,128)(2,1)}, u32[]{:S(2)}, u32[]{:S(2)}) collective-permute-start(bf16[1024,1,1024]{0,2,1:T(8,128)(2,1)} %fusion.7), channel_id=1, source_target_pairs={{0,64},{64,0},{1,65},{65,1},{2,66},{66,2},{3,67},{67,3},{4,68},{68... | collective-permute-start | bytes 6291464 | tf_op jit(solution)/shard_map/ppermute | solution.py:14
  176.3 78.0 %reduce-scatter.5.cloned.1.call-start = ((), (), s32[]{:S(2)}) async-start(), calls=%async_computation.4 | async-start | bytes 2621440 | tf_op jit(solution)/shard_map/reduce_scatter | solution.py:98
Sparse Core Ops, SparseCore 0:
  176.4 22.7 reduce-scatter.6
  222.8 31.4 reduce-scatter.4
where the time goes:
time: 265 us; the launch traced here: 264 us
  waiting for transfers between devices  166 us (63%)
  starting transfers between devices  42.1 us (16%)
  local copies, waits for them, and re-layouts  18.8 us (7%)
  between operations  14.2 us (5%)
  other arithmetic  11.8 us (4%)
  matrix products  11.3 us (4%)
    all_to_all x1, waiting for transfers between devices, shards(): lax.all_to_all(send_rows.reshape(n_exp, exp_dev, 2, cap, width), 'expert'...  90.1 us
    ppermute x2, waiting for transfers between devices, partner(): return lax.ppermute(block, axis, route)  41.9 us
    reduce_scatter x1, waiting for transfers between devices, shards(): lax.psum_scatter((gram_rows(own_grad, own_grad) + far_g).astype(jnp.bfloa...  29.3 us
    all_to_all x1, starting transfers between devices, shards(): lax.all_to_all(send_occ.reshape(n_exp, exp_dev, 2, cap), 'expert', split_...  20.6 us
    all_to_all x1, starting transfers between devices, shards(): lax.all_to_all(send_rows.reshape(n_exp, exp_dev, 2, cap, width), 'expert'...  11.7 us
    ppermute x2, starting transfers between devices, partner(): return lax.ppermute(block, axis, route)  9.84 us
    scatter x1, local copies, waits for them, and re-layouts, shards(): send_occ = jnp.zeros((total,), jnp.bfloat16).at[index].set(jnp.ones(index...  7.58 us
    unnamed x10, local copies, waits for them, and re-layouts  7.17 us
  transfers between devices with their start and end apart: 6, of which 4 were waited for; matrix products, arithmetic and copies ran while one was open for 11% of the time, Pallas kernels for 0%

commit v1 on v0

v1 whole, which is shorter than its diff:
```python
import jax
import jax.numpy as jnp
from jax import lax
from jax.experimental import pallas as pl
from jax.experimental.pallas import tpu as pltpu
from jax.sharding import PartitionSpec as P

NY, NZ, NC, NX = 4, 16, 2, 4
GROUP = NY * NC
HALF = NZ // 2
TOK, TOP, EXPERTS, CAP = 128, 8, 128, 4
WIDTH, HIDDEN = 1024, 768
SLOTS = 2 * CAP
F32, BF16 = jnp.float32, jnp.bfloat16
TN = (((0,), (0,)), ((), ()))


def mm(a, b):
    return jnp.dot(a, b, preferred_element_type=F32)


def iota(shape, dim):
    return lax.broadcasted_iota(jnp.int32, shape, dim)


def kernel(
    routes_ref, weight_ref, hot_ref, grads_ref, inputs_ref,
    grad_out, input_out,
    tokens, table, table_l, table_r, far_inputs, counts, counts_in,
    rows_out, rows_in, gram_g, gram_x,
    gs_out, gs_via, gs_l, gs_r, xs_out, xs_via, xs_l, xs_r,
    tok_send, tok_recv, tab_send, tab_recv, far_sem, cnt_send, cnt_recv,
    row_send, row_recv, gsem_s, gsem_r, xsem_s, xsem_r,
):
    x = lax.axis_index("dp")
    n = lax.axis_index("expert")
    core = lax.rem(n, NC)
    z = lax.rem(n // NC, NZ)
    y = n // (NC * NZ)
    j = y * NC + core

    def expert_at(yy, zz, cc):
        return (yy * NZ + zz) * NC + cc

    z_up = (x, expert_at(y, lax.rem(z + 1, NZ), core))
    z_down = (x, expert_at(y, lax.rem(z + NZ - 1, NZ), core))
    x_up = (lax.rem(x + 1, NX), n)
    x_down = (lax.rem(x + NX - 1, NX), n)

    def flip(k):
        ky, kc = k // NC, k % NC
        if ky == 0:
            yy = y
        elif ky == 1:
            yy = y + 1 - 2 * lax.rem(y, 2)
        elif ky == 2:
            yy = lax.rem(y + 2, 4)
        else:
            yy = 3 - y
        cc = core if kc == 0 else 1 - core
        return yy, cc

    def group_dev(k):
        yy, cc = flip(k)
        return (x, expert_at(yy, z, cc))

    def group_pos(k):
        yy, cc = flip(k)
        return yy * NC + cc

    partners = [z_up, z_down, x_up, x_down] + [group_dev(k) for k in range(1, GROUP)]

    def remote(src, dst, ssem, rsem, dev):
        return pltpu.make_async_remote_copy(
            src_ref=src, dst_ref=dst, send_sem=ssem, recv_sem=rsem,
            device_id=dev, device_id_type=pl.DeviceIdType.MESH,
        )

    barrier = pltpu.get_barrier_semaphore()
    for dev in partners:
        pl.semaphore_signal(barrier, inc=1, device_id=dev, device_id_type=pl.DeviceIdType.MESH)
    pl.semaphore_wait(barrier, len(partners))

    pending = []

    def start(copy):
        copy.start()
        pending.append(copy)
        return copy

    H = TOK // 2

    def token_copy(step, up, half):
        lo = half * H
        base = 0 if up else TOK
        if step == 1:
            src = grads_ref.at[pl.ds(lo, H)]
        else:
            src = tokens.at[step - 2, pl.ds(base + lo, H)]
        if step == HALF:
            dst = tokens.at[HALF - 1, pl.ds(TOK + lo, H)]
        else:
            dst = tokens.at[step - 1, pl.ds(base + lo, H)]
        d = 0 if up else 1
        return remote(
            src, dst, tok_send.at[d, step - 1, half], tok_recv.at[d, step - 1, half],
            z_up if up else z_down,
        )

    tok = {}
    for step in range(1, HALF):
        for half in range(2):
            for up in (True, False):
                tok[step, up, half] = token_copy(step, up, half)
    tok[HALF, True, 0] = token_copy(HALF, True, 0)
    tok[HALF, False, 1] = token_copy(HALF, False, 1)

    def table_copy(step, up):
        buf = table_l if up else table_r
        src = table if step == 1 else buf.at[step - 2]
        d = 0 if up else 1
        return remote(
            src, buf.at[step - 1], tab_send.at[d, step - 1], tab_recv.at[d, step - 1],
            z_up if up else z_down,
        )

    tab = {(s, up): table_copy(s, up) for s in range(1, HALF + 1) for up in (True, False)
           if s < HALF or up}

    for half in range(2):
        for up in (True, False):
            start(tok[1, up, half])

    chosen = routes_ref[...]
    erow = iota((EXPERTS, TOK), 0)
    tcol = iota((EXPERTS, TOK), 1)
    onehot = jnp.zeros((EXPERTS, TOK), F32)
    for k in range(TOP):
        onehot += jnp.where(erow == chosen[k:k + 1, :], 1.0, 0.0)
    earlier = jnp.where(erow < tcol, 1.0, 0.0).astype(BF16)
    before = mm(onehot.astype(BF16), earlier)
    hot = jnp.sum(jnp.where(erow == tcol, jnp.broadcast_to(hot_ref[...].astype(F32), (EXPERTS, TOK)), 0.0),
                  axis=1, keepdims=True)
    limit = jnp.where(hot > 0.5, float(SLOTS), float(CAP))
    ranked = jnp.where(before < limit, before, 1000.0)
    places = []
    for k in range(TOP):
        rank = jnp.sum(jnp.where(erow == chosen[k:k + 1, :], ranked, 0.0), axis=0, keepdims=True)
        slot = chosen[k:k + 1, :].astype(F32) * float(SLOTS) + rank
        places.append(jnp.where(rank < 100.0, slot, -1.0))
    table[0:TOP, :] = jnp.concatenate(places, axis=0)
    table[TOP:2 * TOP, :] = weight_ref[...]

    def pass_table(step):
        for up in (True, False):
            if (step, up) in tab:
                start(tab[step, up])

    def got_table(step):
        for up in (True, False):
            if (step, up) in tab:
                tab[step, up].wait_recv()

    pass_table(1)
    far = start(remote(inputs_ref.at[1], far_inputs, far_sem.at[0], far_sem.at[1], group_dev(4)))

    def advance_table(step):
        got_table(step)
        if step < HALF:
            pass_table(step + 1)

    def advance_tokens(step):
        for half in range(2):
            for up in (True, False):
                if (step, up, half) in tok:
                    tok[step, up, half].wait_recv()
                    if (step + 1, up, half) in tok:
                        start(tok[step + 1, up, half])

    ri = iota((GROUP * 2 * SLOTS, TOK), 0)
    rj = ri // (2 * SLOTS)
    rsrc = lax.rem(ri // SLOTS, 2)
    rslot = (rj // NC) * (NZ * NC * SLOTS) + z * (NC * SLOTS) + lax.rem(rj, NC) * SLOTS + lax.rem(ri, SLOTS)
    want_l = jnp.where(rsrc == 0, rslot, -5).astype(F32)
    want_r = jnp.where(rsrc == 1, rslot, -5).astype(F32)

    def pick(tbl, want):
        sel = jnp.zeros(want.shape, F32)
        wgt = jnp.zeros(want.shape, F32)
        for k in range(TOP):
            hit = want == tbl[k:k + 1, :]
            sel = jnp.where(hit, 1.0, sel)
            wgt = jnp.where(hit, tbl[TOP + k:TOP + k + 1, :], wgt)
        return sel.astype(BF16), wgt

    def dispatch(pair):
        if pair == HALF - 1:
            t_l, t_r = table[...], table_l[HALF - 1]
            g_l = grads_ref[...]
        else:
            t_l, t_r = table_l[pair], table_r[pair]
            g_l = tokens[pair, 0:TOK]
        g_r = tokens[pair, TOK:2 * TOK]
        s_l, w_l = pick(t_l, want_l)
        s_r, w_r = pick(t_r, want_r)
        weight = jnp.sum(w_l + w_r, axis=1, keepdims=True)
        rows = ((mm(s_l, g_l) + mm(s_r, g_r)) * weight).astype(BF16)
        rows_out[pair] = rows.reshape(GROUP, 2 * SLOTS, WIDTH)
        for k in (4, 5, 2, 3, 6, 7, 1):
            start(row_copy(pair, k))
        rows_in[pair, 0] = rows_out[pair, j]

    def row_copy(pair, k):
        return remote(rows_out.at[pair, group_pos(k)], rows_in.at[pair, k],
                      row_send.at[pair, k], row_recv.at[pair, k], group_dev(k))

    def send_counts():
        def one(tbl, zz):
            for jj in range(GROUP):
                lo = (((jj // NC) * NZ + z) * NC + jj % NC) * SLOTS
                lo = lo.astype(F32)
                hit = (tbl >= lo) & (tbl < lo + float(SLOTS))
                counts[jj, pl.ds(zz, 1), :] = jnp.sum(jnp.where(hit, 1.0, 0.0), axis=0, keepdims=True)

        one(table[0:TOP, :], z)
        for s in range(1, HALF + 1):
            one(table_l[s - 1, 0:TOP, :], lax.rem(z + NZ - s, NZ))
            if s < HALF:
                one(table_r[s - 1, 0:TOP, :], lax.rem(z + s, NZ))
        for k in range(1, GROUP):
            start(cnt_copy(k))
        counts_in[j] = counts[j]

    def cnt_copy(k):
        return remote(counts.at[group_pos(k)], counts_in.at[j], cnt_send.at[k], cnt_recv.at[k], group_dev(k))

    def input_gram():
        for k in range(1, GROUP):
            cnt_copy(k).wait_recv()
        per = counts_in[...].reshape(EXPERTS, TOK).astype(BF16)
        ones = jnp.ones((TOK, TOK), BF16)
        total = mm(per, ones).astype(BF16)
        rr = EXPERTS * CAP
        spread = jnp.where(iota((rr, EXPERTS), 0) // CAP == iota((rr, EXPERTS), 1), 1.0, 0.0).astype(BF16)
        mine = mm(spread, total)
        slot = lax.rem(iota((rr, TOK), 0), CAP).astype(F32)
        keep_a = jnp.where(mine > slot, 1.0, 0.0).astype(BF16)
        keep_b = jnp.where(mine > slot + float(CAP), 1.0, 0.0).astype(BF16)
        far.wait_recv()
        block = 256
        for i in range(HIDDEN // block):
            cols = pl.ds(i * block, block)
            ka = jnp.concatenate([keep_a] * (block // TOK), axis=1)
            kb = jnp.concatenate([keep_b] * (block // TOK), axis=1)
            gram_x[cols, :] = lax.dot_general(
                inputs_ref[0, :, cols] * ka, inputs_ref[0], TN, preferred_element_type=F32
            ) + lax.dot_general(far_inputs[:, cols] * kb, far_inputs[...], TN, preferred_element_type=F32)

    class Scatter:
        def __init__(self, gram, rows, out, via, l_in, r_in, ssem, rsem):
            self.gram, self.rows, self.out, self.via = gram, rows, out, via
            self.l_in, self.r_in, self.ssem, self.rsem = l_in, r_in, ssem, rsem
            self.h = rows // 2

        def part(self, blk, half):
            at = pl.multiple_of(blk * self.rows + half * self.h, 32)
            return self.gram[pl.ds(at, self.h), :]

        def copies(self):
            h = self.h
            lo, hi = pl.ds(0, h), pl.ds(h, h)
            ends = [
                (self.via.at[0], x_up), (self.via.at[1], x_down),
                (self.l_in.at[hi], x_up), (self.r_in.at[lo], x_down),
                (self.l_in.at[lo], x_up), (self.r_in.at[hi], x_down),
            ]
            return [remote(self.out.at[i], dst, self.ssem.at[i], self.rsem.at[i], dev)
                    for i, (dst, dev) in enumerate(ends)]

        def first(self):
            self.c = self.copies()
            opposite = lax.rem(x + 2, NX)
            nxt, prv = lax.rem(x + 1, NX), lax.rem(x + NX - 1, NX)
            self.out[0] = self.part(opposite, 0).astype(BF16)
            start(self.c[0])
            self.out[1] = self.part(opposite, 1).astype(BF16)
            start(self.c[1])
            self.out[2] = self.part(nxt, 1).astype(BF16)
            start(self.c[2])
            self.out[3] = self.part(prv, 0).astype(BF16)
            start(self.c[3])

        def second(self):
            nxt, prv = lax.rem(x + 1, NX), lax.rem(x + NX - 1, NX)
            self.c[0].wait_recv()
            self.out[4] = (self.part(nxt, 0) + self.via[0].astype(F32)).astype(BF16)
            start(self.c[4])
            self.c[1].wait_recv()
            self.out[5] = (self.part(prv, 1) + self.via[1].astype(F32)).astype(BF16)
            start(self.c[5])

        def last(self, result):
            factor = 1.0 / (TOK * TOP * NX)
            h = self.h
            lo, hi = pl.ds(0, h), pl.ds(h, h)
            self.c[2].wait_recv()
            self.c[3].wait_recv()
            self.c[4].wait_recv()
            result[lo, :] = (self.part(x, 0) + self.l_in[lo].astype(F32) + self.r_in[lo].astype(F32)) * factor
            self.c[5].wait_recv()
            result[hi, :] = (self.part(x, 1) + self.l_in[hi].astype(F32) + self.r_in[hi].astype(F32)) * factor

    xs = Scatter(gram_x, HIDDEN // NX, xs_out, xs_via, xs_l, xs_r, xsem_s, xsem_r)
    gs = Scatter(gram_g, WIDTH // NX, gs_out, gs_via, gs_l, gs_r, gsem_s, gsem_r)

    def gram_part(first_pair, pairs, fresh):
        for p in range(first_pair, first_pair + pairs):
            for k in range(1, GROUP):
                row_copy(p, k).wait_recv()
        kk = pairs * GROUP * 2 * SLOTS

        def body(i, carry):
            at = pl.multiple_of(i * 256, 256)
            a = rows_in[first_pair:first_pair + pairs, :, :, pl.ds(at, 256)].reshape(kk, 256)
            b = rows_in[first_pair:first_pair + pairs].reshape(kk, WIDTH)
            r = lax.dot_general(a, b, TN, preferred_element_type=F32)
            if fresh:
                gram_g[pl.ds(at, 256), :] = r
            else:
                gram_g[pl.ds(at, 256), :] += r
            return carry

        lax.fori_loop(0, WIDTH // 256, body, 0)

    advance_table(1)
    advance_table(2)
    advance_table(3)
    advance_tokens(1)
    advance_table(4)
    advance_table(5)
    advance_table(6)
    advance_tokens(2)
    dispatch(0)
    advance_table(7)
    advance_table(8)
    send_counts()
    advance_tokens(3)
    dispatch(1)
    advance_tokens(4)
    dispatch(2)
    input_gram()
    xs.first()
    advance_tokens(5)
    dispatch(3)
    gram_part(0, 2, True)
    advance_tokens(6)
    xs.second()
    dispatch(4)
    advance_tokens(7)
    dispatch(5)
    gram_part(2, 2, False)
    xs.last(input_out)
    dispatch(6)
    gram_part(4, 2, False)
    advance_tokens(8)
    dispatch(7)
    gram_part(6, 2, False)
    gs.first()
    gs.second()
    gs.last(grad_out)
    for copy in pending:
        copy.wait_send()


def shards(grads, route_weight, routes, hot, expert_inputs):
    inputs = expert_inputs.reshape(NY, NZ, NC, 2, CAP, HIDDEN)
    inputs = inputs.transpose(3, 0, 2, 1, 4, 5).reshape(2, EXPERTS * CAP, HIDDEN)
    vmem = pl.BlockSpec(memory_space=pltpu.VMEM)
    dma = pltpu.SemaphoreType.DMA
    hg, hx = WIDTH // NX // 2, HIDDEN // NX // 2
    grad_rows, input_rows = pl.pallas_call(
        kernel,
        out_shape=(
            jax.ShapeDtypeStruct((WIDTH // NX, WIDTH), F32),
            jax.ShapeDtypeStruct((HIDDEN // NX, HIDDEN), F32),
        ),
        in_specs=[vmem] * 5,
        out_specs=(vmem, vmem),
        scratch_shapes=[
            pltpu.VMEM((HALF, 2 * TOK, WIDTH), BF16),
            pltpu.VMEM((2 * TOP, TOK), F32),
            pltpu.VMEM((HALF, 2 * TOP, TOK), F32),
            pltpu.VMEM((HALF, 2 * TOP, TOK), F32),
            pltpu.VMEM((EXPERTS * CAP, HIDDEN), BF16),
            pltpu.VMEM((GROUP, NZ, TOK), F32),
            pltpu.VMEM((GROUP, NZ, TOK), F32),
            pltpu.VMEM((HALF, GROUP, 2 * SLOTS, WIDTH), BF16),
            pltpu.VMEM((HALF, GROUP, 2 * SLOTS, WIDTH), BF16),
            pltpu.VMEM((WIDTH, WIDTH), F32),
            pltpu.VMEM((HIDDEN, HIDDEN), F32),
            pltpu.VMEM((6, hg, WIDTH), BF16),
            pltpu.VMEM((2, hg, WIDTH), BF16),
            pltpu.VMEM((2 * hg, WIDTH), BF16),
            pltpu.VMEM((2 * hg, WIDTH), BF16),
            pltpu.VMEM((6, hx, HIDDEN), BF16),
            pltpu.VMEM((2, hx, HIDDEN), BF16),
            pltpu.VMEM((2 * hx, HIDDEN), BF16),
            pltpu.VMEM((2 * hx, HIDDEN), BF16),
            dma((2, HALF, 2)), dma((2, HALF, 2)),
            dma((2, HALF)), dma((2, HALF)),
            dma((2,)),
            dma((GROUP,)), dma((GROUP,)),
            dma((HALF, GROUP)), dma((HALF, GROUP)),
            dma((6,)), dma((6,)), dma((6,)), dma((6,)),
        ],
        compiler_params=pltpu.CompilerParams(
            collective_id=0, has_side_effects=True, vmem_limit_bytes=48 * 1024 * 1024
        ),
    )(routes.T, route_weight.T, hot.reshape(1, EXPERTS), grads, inputs)
    return input_rows[:, None, :], grad_rows[:, None, :]


def solution(mesh):
    return jax.shard_map(
        shards,
        mesh=mesh,
        in_specs=(
            P(("dp", "expert"), None),
            P(("dp", "expert"), None),
            P(("dp", "expert"), None),
            P(),
            P("dp", "expert", None, None, None, None, None),
        ),
        out_specs=(P("dp", "expert", None), P("dp", "expert", None)),
        check_vma=False,
    )
```

time: 265 us -> 112 us (0.42)
  waiting for transfers between devices: 166 us -> 0 us
  Pallas kernels: 0 us -> 105 us
  starting transfers between devices: 42.1 us -> 0 us
  between operations: 14.2 us -> 0.69 us
  local copies, waits for them, and re-layouts: 18.8 us -> 6.53 us
  other arithmetic: 11.8 us -> 0 us
  matrix products: 11.3 us -> 0 us
    pallas_call x0 -> x1, Pallas kernels: none -> 105 us  [shards(): pl.pallas_call(kernel, out_shape=(jax.ShapeDtypeStruct((WIDTH // NX, WIDT...]
    all_to_all x2 -> x0, waiting for transfers between devices: 94.6 us -> none  [the longest x1 90.1 us: shards(): lax.all_to_all(send_rows.reshape(n_exp, exp_dev, 2, cap, width), 'expert'...]
    ppermute x2 -> x0, waiting for transfers between devices: 41.9 us -> none  [partner(): return lax.ppermute(block, axis, route)]
    all_to_all x2 -> x0, starting transfers between devices: 32.2 us -> none  [the longest x1 20.6 us: shards(): lax.all_to_all(send_occ.reshape(n_exp, exp_dev, 2, cap), 'expert', split_...]
    reduce_scatter x1 -> x0, waiting for transfers between devices: 29.3 us -> none  [shards(): lax.psum_scatter((gram_rows(own_grad, own_grad) + far_g).astype(jnp.bfloa...]
    dot_general x5 -> x0, matrix products: 11.3 us -> none  [the longest x2 6.52 us: gram_rows(): jnp.einsum('nlcf,nlcg->flg', left, right, preferred_element_type=jnp.floa...]
    ppermute x2 -> x0, starting transfers between devices: 9.84 us -> none  [partner(): return lax.ppermute(block, axis, route)]
    scatter x1 -> x0, local copies, waits for them, and re-layouts: 7.58 us -> none  [shards(): send_occ = jnp.zeros((total,), jnp.bfloat16).at[index].set(jnp.ones(index...]
  transfers between devices with their start and end apart: 6 -> 0, of which waited for: 4 -> 0; matrix products, arithmetic and copies ran while one was open for 11% -> 0% of each run, Pallas kernels for 0% -> 0%
where the time goes in v1:
time: 112 us
  Pallas kernels  105 us (94%)
  local copies, waits for them, and re-layouts  6.53 us (6%)
    pallas_call x1, Pallas kernels, shards(): pl.pallas_call(kernel, out_shape=(jax.ShapeDtypeStruct((WIDTH // NX, WIDT...  105 us
    unnamed x10, local copies, waits for them, and re-layouts  3.99 us

profile of v1, /device:TPU:1, one launch (start us, length us, event | category | flops | bytes accessed | tf_op | source)
XLA Modules:
  0.0 111.8 jit_solution(2955423880917382948)
XLA Ops:
  0.6 2.1 %copy.11 = bf16[4,16,2,2,4,768]{5,4,1,2,0,3:T(4,128)(2,1)S(1)} copy(bf16[4,16,2,2,4,768]{5,4,3,2,1,0:T(4,128)(2,1)} %bitcast.15) | data formatting | bytes 3145728 | tf_op jit(solution)/shard_map/reshape | solution.py:376
  2.8 0.0 copy-start
  2.8 0.0 copy-start.1
  2.8 0.0 copy-start.2
  2.8 0.0 copy-start.3
  2.8 0.4 reshape.15.inputs_ref
  3.2 0.5 copy-done
  3.7 0.0 copy-done.1
  3.7 0.0 copy-done.2
  3.7 0.0 copy-done.3
  3.7 104.6 %shard_map.68 = (f32[256,1024]{1,0:T(8,128)S(1)}, f32[192,768]{1,0:T(8,128)S(1)}) custom-call(s32[8,128]{1,0:T(8,128)S(1)} %bitcast.11, f32[8,128]{1,0:T(8,128)S(1)} %bitcast.12, s32[1,128]{1,0:T(1,128)S(1)} %bitcast.13, bf16[128,1024]{1,0:T(8,128)(2,1)S(1)} %copy-done, bf16[2,512,768]{2,1,0:T(8,128)(2,1)S(1)} %reshape.15.inputs_ref), custom_call_target="tpu_custom_call" | custom-call | tf_op jit(solution)/shard_map/pallas_call | solution.py:381
  108.3 1.4 %copy.8 = f32[192,1,768]{2,1,0:T(1,128)} copy(f32[192,1,768]{2,0,1:T(8,128)S(1)} %bitcast.10) | data formatting | bytes 1179648
  109.8 2.0 %copy.9 = f32[256,1,1024]{2,1,0:T(1,128)} copy(f32[256,1,1024]{2,0,1:T(8,128)S(1)} %bitcast.9) | data formatting | bytes 2097152
Async XLA Ops:
  2.8 1.0 copy-start
  2.8 0.9 copy-start.1
  2.8 0.9 copy-start.2
  2.8 0.9 copy-start.3

commit v2 on v1

v2 whole, which is shorter than its diff:
```python
import jax
import jax.numpy as jnp
from jax import lax
from jax.experimental import pallas as pl
from jax.experimental.pallas import tpu as pltpu
from jax.sharding import PartitionSpec as P

NY, NZ, NC, NX = 4, 16, 2, 4
GROUP = NY * NC
HALF = NZ // 2
TOK, TOP, EXPERTS, CAP = 128, 8, 128, 4
WIDTH, HIDDEN = 1024, 768
SLOTS = 2 * CAP
F32, BF16 = jnp.float32, jnp.bfloat16
TN = (((0,), (0,)), ((), ()))


def mm(a, b):
    return jnp.dot(a, b, preferred_element_type=F32)


def iota(shape, dim):
    return lax.broadcasted_iota(jnp.int32, shape, dim)


def kernel(
    routes_ref, weight_ref, hot_ref, grads_ref, inputs_ref,
    grad_out, input_out,
    tokens, table, table_in, keep, counts, counts_in,
    rows_out, rows_in, gram_g, gram_o, gram_r, mine, theirs,
    gs_out, gs_via, gs_l, gs_r, os_out, os_via, os_l, os_r, rs_out, rs_via, rs_l, rs_r,
    tok_send, tok_recv, tab_send, tab_recv, far_sem, cnt_send, cnt_recv,
    row_send, row_recv, gsem_s, gsem_r, osem_s, osem_r, rsem_s, rsem_r,
):
    x = lax.axis_index("dp")
    n = lax.axis_index("expert")
    core = lax.rem(n, NC)
    z = lax.rem(n // NC, NZ)
    y = n // (NC * NZ)
    j = y * NC + core

    def expert_at(yy, zz, cc):
        return (yy * NZ + zz) * NC + cc

    def z_dev(d):
        return (x, expert_at(y, lax.rem(z + d, NZ), core))

    z_up, z_down = z_dev(1), z_dev(NZ - 1)
    x_up = (lax.rem(x + 1, NX), n)
    x_down = (lax.rem(x + NX - 1, NX), n)

    def flip(k):
        ky, kc = k // NC, k % NC
        if ky == 0:
            yy = y
        elif ky == 1:
            yy = y + 1 - 2 * lax.rem(y, 2)
        elif ky == 2:
            yy = lax.rem(y + 2, 4)
        else:
            yy = 3 - y
        cc = core if kc == 0 else 1 - core
        return yy, cc

    def group_dev(k):
        yy, cc = flip(k)
        return (x, expert_at(yy, z, cc))

    def group_pos(k):
        yy, cc = flip(k)
        return yy * NC + cc

    partners = [z_dev(d) for d in range(1, NZ)] + [x_up, x_down] + [group_dev(k) for k in range(1, GROUP)]

    def remote(src, dst, ssem, rsem, dev):
        return pltpu.make_async_remote_copy(
            src_ref=src, dst_ref=dst, send_sem=ssem, recv_sem=rsem,
            device_id=dev, device_id_type=pl.DeviceIdType.MESH,
        )

    barrier = pltpu.get_barrier_semaphore()
    for dev in partners:
        pl.semaphore_signal(barrier, inc=1, device_id=dev, device_id_type=pl.DeviceIdType.MESH)
    pending = []

    def start(copy):
        copy.start()
        pending.append(copy)
        return copy

    H = TOK // 2

    def token_copy(step, up, half):
        lo = half * H
        base = 0 if up else TOK
        if step == 1:
            src = grads_ref.at[pl.ds(lo, H)]
        else:
            src = tokens.at[step - 2, pl.ds(base + lo, H)]
        if step == HALF:
            dst = tokens.at[HALF - 1, pl.ds(TOK + lo, H)]
        else:
            dst = tokens.at[step - 1, pl.ds(base + lo, H)]
        d = 0 if up else 1
        return remote(
            src, dst, tok_send.at[d, step - 1, half], tok_recv.at[d, step - 1, half],
            z_up if up else z_down,
        )

    tok = {}
    for step in range(1, HALF):
        for half in range(2):
            for up in (True, False):
                tok[step, up, half] = token_copy(step, up, half)
    tok[HALF, True, 0] = token_copy(HALF, True, 0)
    tok[HALF, False, 1] = token_copy(HALF, False, 1)

    chosen = routes_ref[...]
    erow = iota((EXPERTS, TOK), 0)
    tcol = iota((EXPERTS, TOK), 1)
    onehot = jnp.zeros((EXPERTS, TOK), F32)
    for k in range(TOP):
        onehot += jnp.where(erow == chosen[k:k + 1, :], 1.0, 0.0)
    earlier = jnp.where(erow < tcol, 1.0, 0.0).astype(BF16)
    before = mm(onehot.astype(BF16), earlier)
    hot = jnp.sum(jnp.where(erow == tcol, jnp.broadcast_to(hot_ref[...].astype(F32), (EXPERTS, TOK)), 0.0),
                  axis=1, keepdims=True)
    limit = jnp.where(hot > 0.5, float(SLOTS), float(CAP))
    ranked = jnp.where(before < limit, before, 1000.0)
    zrow = iota((NZ, TOK), 0)
    irow = lax.rem(iota((TOK, TOK), 0), GROUP * SLOTS).astype(F32)
    token = (iota((NZ, TOK), 1) + 1).astype(F32)
    lefts, rights = [], []
    for k in range(TOP):
        e = chosen[k:k + 1, :]
        rank = jnp.sum(jnp.where(erow == e, ranked, 0.0), axis=0, keepdims=True)
        at = (((e // (NZ * NC)) * NC + lax.rem(e, NC)) * SLOTS).astype(F32) + rank
        here = zrow == lax.rem(e // NC, NZ)
        w = weight_ref[k:k + 1, :]
        w1 = w.astype(BF16).astype(F32)
        w2 = (w - w1).astype(BF16).astype(F32)
        w3 = w - w1 - w2
        lefts.append(jnp.concatenate(
            [jnp.where(here, v, 0.0) for v in (token, w1, w2, w3)], axis=0).astype(BF16))
        rights.append(jnp.where(irow == at, 1.0, 0.0).astype(BF16))
    found = lax.dot_general(jnp.concatenate(lefts, axis=1), jnp.concatenate(rights, axis=1),
                            (((1,), (1,)), ((), ())), preferred_element_type=F32)
    weights = found[NZ:2 * NZ] + found[2 * NZ:3 * NZ] + found[3 * NZ:4 * NZ]
    listing = jnp.where(iota((NZ, TOK), 1) < GROUP * SLOTS, found[0:NZ] - 1.0, weights)
    for zz in range(NZ):
        table[zz] = listing[zz:zz + 1, :]

    def table_copy(d):
        return remote(table.at[lax.rem(z + d, NZ)], table_in.at[z], tab_send.at[d], tab_recv.at[d], z_dev(d))

    pl.semaphore_wait(barrier, len(partners))
    for d in (1, 15, 2, 14, 3, 13, 4, 12, 5, 11, 6, 10, 7, 9, 8):
        start(table_copy(d))
    for half in range(2):
        for up in (True, False):
            start(tok[1, up, half])
    table_in[z] = table[z]

    def advance(step, half):
        for up in (True, False):
            if (step, up, half) in tok:
                tok[step, up, half].wait_recv()
                if (step + 1, up, half) in tok:
                    start(tok[step + 1, up, half])

    ri = iota((GROUP * 2 * SLOTS, TOK), 0)
    rl = iota((GROUP * 2 * SLOTS, TOK), 1)
    from_l = lax.rem(ri // SLOTS, 2) == 0
    rslot = (ri // (2 * SLOTS)) * SLOTS + lax.rem(ri, SLOTS)
    at_token = rl == rslot
    at_weight = rl == rslot + GROUP * SLOTS
    lane = rl.astype(F32)

    def dispatch(pair):
        if pair == HALF - 1:
            t_l, t_r = table_in[z], table_in[lax.rem(z + HALF, NZ)]
            g_l = grads_ref[...]
        else:
            t_l, t_r = table_in[lax.rem(z + NZ - 1 - pair, NZ)], table_in[lax.rem(z + 1 + pair, NZ)]
            g_l = tokens[pair, 0:TOK]
        g_r = tokens[pair, TOK:2 * TOK]
        both = jnp.where(from_l, t_l, t_r)
        token_of = jnp.sum(jnp.where(at_token, both, 0.0), axis=1, keepdims=True)
        weight = jnp.sum(jnp.where(at_weight, both, 0.0), axis=1, keepdims=True)
        hit = jnp.where(lane == token_of, 1.0, 0.0)
        s_l = jnp.where(from_l, hit, 0.0).astype(BF16)
        s_r = jnp.where(from_l, 0.0, hit).astype(BF16)
        rows = ((mm(s_l, g_l) + mm(s_r, g_r)) * weight).astype(BF16)
        rows_out[pair] = rows.reshape(GROUP, 2 * SLOTS, WIDTH)
        for k in (4, 5, 2, 3, 6, 7, 1):
            start(row_copy(pair, k))
        rows_in[pair, 0] = rows_out[pair, j]

    def row_copy(pair, k):
        return remote(rows_out.at[pair, group_pos(k)], rows_in.at[pair, k],
                      row_send.at[pair, k], row_recv.at[pair, k], group_dev(k))

    def send_counts():
        for d in range(1, NZ):
            table_copy(d).wait_recv()
        used = jnp.where(table_in[...].reshape(NZ, TOK) >= 0.0, 1.0, 0.0).astype(BF16)
        src = iota((TOK, TOK), 0)
        hosted = iota((TOK, TOK), 1) >= TOK // 2
        for jj in range(GROUP):
            want = jnp.where(hosted, jj ^ (GROUP // 2), jj)
            counts[jj] = mm(used, jnp.where(src // SLOTS == want, 1.0, 0.0).astype(BF16))
        for k in range(1, GROUP):
            start(cnt_copy(k))
        counts_in[j] = counts[j]

    def cnt_copy(k):
        return remote(counts.at[group_pos(k)], counts_in.at[j], cnt_send.at[k], cnt_recv.at[k], group_dev(k))

    def masks():
        for k in range(1, GROUP):
            cnt_copy(k).wait_recv()
        per = counts_in[...].reshape(EXPERTS, TOK).astype(BF16)
        rr = EXPERTS * SLOTS
        source = iota((rr, EXPERTS), 0) // SLOTS
        m = iota((rr, EXPERTS), 1)
        place = ((m // (NC * NZ)) * NZ + lax.rem(m, NZ)) * NC + lax.rem(m // NZ, NC)
        spread = jnp.where(source == place, 1.0, 0.0).astype(BF16)
        each = mm(spread, per).astype(BF16)
        slot = lax.rem(iota((rr, TOK), 0), SLOTS)
        for i in range(2):
            pickone = jnp.where(iota((TOK, TOK), 0) == i * (TOK // 2), 1.0, 0.0).astype(BF16)
            many = mm(each, pickone)
            good = (many > slot.astype(F32)) & ((slot >= CAP) if i else (slot < CAP))
            keep[i] = jnp.where(good, 1.0, 0.0).astype(BF16)

    def input_gram(gram, which, i):
        block = 256
        cols = pl.ds(i * block, block)
        kept = jnp.concatenate([keep[which]] * (block // TOK), axis=1)
        gram[cols, :] = lax.dot_general(
            inputs_ref[:, cols] * kept, inputs_ref[...], TN, preferred_element_type=F32)

    class Scatter:
        def __init__(self, gram, rows, out, via, l_in, r_in, ssem, rsem):
            self.gram, self.rows, self.out, self.via = gram, rows, out, via
            self.l_in, self.r_in, self.ssem, self.rsem = l_in, r_in, ssem, rsem
            self.h = rows // 2

        def part(self, blk, half):
            at = pl.multiple_of(blk * self.rows + half * self.h, 32)
            return self.gram[pl.ds(at, self.h), :]

        def copies(self):
            h = self.h
            lo, hi = pl.ds(0, h), pl.ds(h, h)
            ends = [
                (self.via.at[0], x_up), (self.via.at[1], x_down),
                (self.l_in.at[hi], x_up), (self.r_in.at[lo], x_down),
                (self.l_in.at[lo], x_up), (self.r_in.at[hi], x_down),
            ]
            return [remote(self.out.at[i], dst, self.ssem.at[i], self.rsem.at[i], dev)
                    for i, (dst, dev) in enumerate(ends)]

        def first(self, ready=None):
            self.c = self.copies()
            opposite = lax.rem(x + 2, NX)
            nxt, prv = lax.rem(x + 1, NX), lax.rem(x + NX - 1, NX)
            if ready is not None:
                ready(opposite)
            self.out[0] = self.part(opposite, 0).astype(BF16)
            start(self.c[0])
            self.out[1] = self.part(opposite, 1).astype(BF16)
            start(self.c[1])
            if ready is not None:
                ready(nxt)
            self.out[2] = self.part(nxt, 1).astype(BF16)
            start(self.c[2])
            if ready is not None:
                ready(prv)
            self.out[3] = self.part(prv, 0).astype(BF16)
            start(self.c[3])
            if ready is not None:
                ready(x)

        def second(self):
            nxt, prv = lax.rem(x + 1, NX), lax.rem(x + NX - 1, NX)
            self.c[0].wait_recv()
            self.out[4] = (self.part(nxt, 0) + self.via[0].astype(F32)).astype(BF16)
            start(self.c[4])
            self.c[1].wait_recv()
            self.out[5] = (self.part(prv, 1) + self.via[1].astype(F32)).astype(BF16)
            start(self.c[5])

        def last(self, put):
            h = self.h
            lo, hi = pl.ds(0, h), pl.ds(h, h)
            self.c[2].wait_recv()
            self.c[3].wait_recv()
            self.c[4].wait_recv()
            put(lo, self.part(x, 0) + self.l_in[lo].astype(F32) + self.r_in[lo].astype(F32))
            self.c[5].wait_recv()
            put(hi, self.part(x, 1) + self.l_in[hi].astype(F32) + self.r_in[hi].astype(F32))

    factor = 1.0 / (TOK * TOP * NX)

    own = Scatter(gram_o, HIDDEN // NX, os_out, os_via, os_l, os_r, osem_s, osem_r)
    rep = Scatter(gram_r, HIDDEN // NX, rs_out, rs_via, rs_l, rs_r, rsem_s, rsem_r)
    gs = Scatter(gram_g, WIDTH // NX, gs_out, gs_via, gs_l, gs_r, gsem_s, gsem_r)

    def rows_ready(first_pair, pairs):
        for p in range(first_pair, first_pair + pairs):
            for k in range(1, GROUP):
                row_copy(p, k).wait_recv()

    def gram_rows(first_pair, pairs, blk, fresh):
        kk = pairs * GROUP * 2 * SLOTS
        at = pl.multiple_of(blk * 256, 256)
        a = rows_in[first_pair:first_pair + pairs, :, :, pl.ds(at, 256)].reshape(kk, 256)
        b = rows_in[first_pair:first_pair + pairs].reshape(kk, WIDTH)
        r = lax.dot_general(a, b, TN, preferred_element_type=F32)
        if fresh:
            gram_g[pl.ds(at, 256), :] = r
        else:
            gram_g[pl.ds(at, 256), :] += r

    def gram_part(first_pair, pairs, fresh):
        rows_ready(first_pair, pairs)

        def body(i, carry):
            gram_rows(first_pair, pairs, i, fresh)
            return carry

        lax.fori_loop(0, WIDTH // 256, body, 0)

    far = remote(mine, theirs, far_sem.at[0], far_sem.at[1], group_dev(4))

    def put_mine(at, value):
        mine[at, :] = value.astype(BF16)

    def put_input(at, value):
        input_out[at, :] = (value + theirs[at, :].astype(F32)) * factor

    def put_grad(at, value):
        grad_out[at, :] = value * factor

    advance(1, 0)
    send_counts()
    advance(1, 1)
    dispatch(0)
    advance(2, 0)
    masks()
    input_gram(gram_r, 1, 0)
    advance(2, 1)
    dispatch(1)
    input_gram(gram_r, 1, 1)
    advance(3, 0)
    input_gram(gram_r, 1, 2)
    rep.first()
    advance(3, 1)
    dispatch(2)
    input_gram(gram_o, 0, 0)
    advance(4, 0)
    input_gram(gram_o, 0, 1)
    input_gram(gram_o, 0, 2)
    advance(4, 1)
    dispatch(3)
    rep.second()
    advance(5, 0)
    own.first()
    rep.last(put_mine)
    start(far)
    advance(5, 1)
    dispatch(4)
    advance(6, 0)
    gram_part(0, 2, True)
    advance(6, 1)
    dispatch(5)
    own.second()
    advance(7, 0)
    gram_part(2, 2, False)
    advance(7, 1)
    dispatch(6)
    gram_part(4, 2, False)
    far.wait_recv()
    own.last(put_input)
    advance(8, 0)
    advance(8, 1)
    dispatch(7)
    rows_ready(6, 2)
    gs.first(lambda blk: gram_rows(6, 2, blk, False))
    gs.second()
    gs.last(put_grad)
    for copy in pending:
        copy.wait_send()


def shards(grads, route_weight, routes, hot, expert_inputs):
    inputs = expert_inputs.reshape(EXPERTS * SLOTS, HIDDEN)
    vmem = pl.BlockSpec(memory_space=pltpu.VMEM)
    dma = pltpu.SemaphoreType.DMA
    hg, hx = WIDTH // NX // 2, HIDDEN // NX // 2
    grad_rows, input_rows = pl.pallas_call(
        kernel,
        out_shape=(
            jax.ShapeDtypeStruct((WIDTH // NX, WIDTH), F32),
            jax.ShapeDtypeStruct((HIDDEN // NX, HIDDEN), F32),
        ),
        in_specs=[vmem] * 5,
        out_specs=(vmem, vmem),
        scratch_shapes=[
            pltpu.VMEM((HALF, 2 * TOK, WIDTH), BF16),
            pltpu.VMEM((NZ, 1, TOK), F32),
            pltpu.VMEM((NZ, 1, TOK), F32),
            pltpu.VMEM((2, EXPERTS * SLOTS, TOK), BF16),
            pltpu.VMEM((GROUP, NZ, TOK), F32),
            pltpu.VMEM((GROUP, NZ, TOK), F32),
            pltpu.VMEM((HALF, GROUP, 2 * SLOTS, WIDTH), BF16),
            pltpu.VMEM((HALF, GROUP, 2 * SLOTS, WIDTH), BF16),
            pltpu.VMEM((WIDTH, WIDTH), F32),
            pltpu.VMEM((HIDDEN, HIDDEN), F32),
            pltpu.VMEM((HIDDEN, HIDDEN), F32),
            pltpu.VMEM((2 * hx, HIDDEN), BF16),
            pltpu.VMEM((2 * hx, HIDDEN), BF16),
            pltpu.VMEM((6, hg, WIDTH), BF16),
            pltpu.VMEM((2, hg, WIDTH), BF16),
            pltpu.VMEM((2 * hg, WIDTH), BF16),
            pltpu.VMEM((2 * hg, WIDTH), BF16),
            pltpu.VMEM((6, hx, HIDDEN), BF16),
            pltpu.VMEM((2, hx, HIDDEN), BF16),
            pltpu.VMEM((2 * hx, HIDDEN), BF16),
            pltpu.VMEM((2 * hx, HIDDEN), BF16),
            pltpu.VMEM((6, hx, HIDDEN), BF16),
            pltpu.VMEM((2, hx, HIDDEN), BF16),
            pltpu.VMEM((2 * hx, HIDDEN), BF16),
            pltpu.VMEM((2 * hx, HIDDEN), BF16),
            dma((2, HALF, 2)), dma((2, HALF, 2)),
            dma((NZ,)), dma((NZ,)),
            dma((2,)),
            dma((GROUP,)), dma((GROUP,)),
            dma((HALF, GROUP)), dma((HALF, GROUP)),
            dma((6,)), dma((6,)), dma((6,)), dma((6,)), dma((6,)), dma((6,)),
        ],
        compiler_params=pltpu.CompilerParams(
            collective_id=0, has_side_effects=True, vmem_limit_bytes=48 * 1024 * 1024
        ),
    )(routes.T, route_weight.T, hot.reshape(1, EXPERTS), grads, inputs)
    return input_rows[:, None, :], grad_rows[:, None, :]


def solution(mesh):
    return jax.shard_map(
        shards,
        mesh=mesh,
        in_specs=(
            P(("dp", "expert"), None),
            P(("dp", "expert"), None),
            P(("dp", "expert"), None),
            P(),
            P("dp", "expert", None, None, None, None, None),
        ),
        out_specs=(P("dp", "expert", None), P("dp", "expert", None)),
        check_vma=False,
    )
```

time: 112 us -> 98.7 us (0.88)
  Pallas kernels: 105 us -> 91.5 us
    pallas_call x1, Pallas kernels: 105 us -> 91.5 us  [shards(): pl.pallas_call(kernel, out_shape=(jax.ShapeDtypeStruct((WIDTH // NX, WIDT...]
    reshape x2 -> x1, local copies, waits for them, and re-layouts: 2.54 us -> 2.78 us  [shards(): inputs = expert_inputs.reshape(EXPERTS * SLOTS, HIDDEN)]
where the time goes in v2:
time: 98.7 us; the launch traced here: 98.5 us
  Pallas kernels  91.5 us (93%)
  local copies, waits for them, and re-layouts  6.27 us (6%)
    pallas_call x1, Pallas kernels, shards(): pl.pallas_call(kernel, out_shape=(jax.ShapeDtypeStruct((WIDTH // NX, WIDT...  91.5 us
    unnamed x10, local copies, waits for them, and re-layouts  3.49 us
    reshape x1, local copies, waits for them, and re-layouts, shards(): inputs = expert_inputs.reshape(EXPERTS * SLOTS, HIDDEN)  2.78 us

profile of v2, /device:TPU:1, one launch (start us, length us, event | category | flops | bytes accessed | tf_op | source)
XLA Modules:
  0.0 98.5 jit_solution(12388502109452142067)
XLA Ops:
  0.6 0.0 copy-start
  0.6 0.0 copy-start.1
  0.7 0.0 copy-start.2
  0.7 0.0 copy-start.3
  0.7 2.8 %reshape.11.inputs_ref = bf16[1024,768]{1,0:T(8,128)(2,1)S(1)} reshape(bf16[1,1,128,1,2,4,768]{6,5,4,3,2,1,0:T(4,128)(2,1)} %param.9) | data formatting | bytes 3145728 | tf_op jit(solution)/shard_map/reshape | solution.py:398
  3.5 0.0 copy-done
  3.5 0.0 copy-done.1
  3.5 0.0 copy-done.2
  3.5 0.0 copy-done.3
  3.5 91.5 %shard_map.68 = (f32[256,1024]{1,0:T(8,128)S(1)}, f32[192,768]{1,0:T(8,128)S(1)}) custom-call(s32[8,128]{1,0:T(8,128)S(1)} %bitcast.7, f32[8,128]{1,0:T(8,128)S(1)} %bitcast.8, s32[1,128]{1,0:T(1,128)S(1)} %bitcast.9, bf16[128,1024]{1,0:T(8,128)(2,1)S(1)} %copy-done, bf16[1024,768]{1,0:T(8,128)(2,1)S(1)} %reshape.11.inputs_ref), custom_call_target="tpu_custom_call" | custom-call | tf_op jit(solution)/shard_map/pallas_call | solution.py:402
  95.0 1.4 %copy.7 = f32[192,1,768]{2,1,0:T(1,128)} copy(f32[192,1,768]{2,0,1:T(8,128)S(1)} %bitcast.6) | data formatting | bytes 1179648
  96.5 2.0 %copy.8 = f32[256,1,1024]{2,1,0:T(1,128)} copy(f32[256,1,1024]{2,0,1:T(8,128)S(1)} %bitcast.5) | data formatting | bytes 2097152
Async XLA Ops:
  0.6 2.8 %copy-start = (bf16[128,1024]{1,0:T(8,128)(2,1)S(1)}, bf16[128,1024]{1,0:T(8,128)(2,1)}, u32[]{:S(2)}) copy-start(bf16[128,1024]{1,0:T(8,128)(2,1)} %grads_ref.1) | copy-start | bytes 786436
  0.6 2.8 %copy-start.1 = (s32[128,8]{0,1:T(8,128)S(1)}, s32[128,8]{0,1:T(8,128)}, u32[]{:S(2)}) copy-start(s32[128,8]{0,1:T(8,128)} %param.7) | copy-start | bytes 12292
  0.7 2.8 %copy-start.2 = (f32[128,8]{0,1:T(8,128)S(1)}, f32[128,8]{0,1:T(8,128)}, u32[]{:S(2)}) copy-start(f32[128,8]{0,1:T(8,128)} %param.6) | copy-start | bytes 12292
  0.7 2.8 %copy-start.3 = (s32[128]{0:T(128)S(1)}, s32[128]{0:T(128)}, u32[]{:S(2)}) copy-start(s32[128]{0:T(128)} %param.8) | copy-start | bytes 1540

commit v3 on v2

--- a/solution.py
+++ b/solution.py
@@ -24,9 +24,9 @@
 
 
 def kernel(
-    routes_ref, weight_ref, hot_ref, grads_ref, inputs_ref,
-    grad_out, input_out,
-    tokens, table, table_in, keep, counts, counts_in,
+    routes_hbm, weight_hbm, hot_hbm, grads_hbm, inputs_hbm,
+    grad_hbm, input_hbm,
+    routes_ref, weight_ref, hot_ref, grads_ref, grad_out, input_out, out_sem, inputs_raw, inputs_ref, in_sem, tokens, table, table_in, keep, counts, counts_in,
     rows_out, rows_in, gram_g, gram_o, gram_r, mine, theirs,
     gs_out, gs_via, gs_l, gs_r, os_out, os_via, os_l, os_r, rs_out, rs_via, rs_l, rs_r,
     tok_send, tok_recv, tab_send, tab_recv, far_sem, cnt_send, cnt_recv,
@@ -78,6 +78,15 @@
             device_id=dev, device_id_type=pl.DeviceIdType.MESH,
         )
 
+    loads = [
+        pltpu.make_async_copy(a, b, in_sem.at[i])
+        for i, (a, b) in enumerate([
+            (grads_hbm, grads_ref), (routes_hbm, routes_ref), (weight_hbm, weight_ref), (hot_hbm, hot_ref),
+            (inputs_hbm, inputs_raw),
+        ])
+    ]
+    for load in loads:
+        load.start()
     barrier = pltpu.get_barrier_semaphore()
     for dev in partners:
         pl.semaphore_signal(barrier, inc=1, device_id=dev, device_id_type=pl.DeviceIdType.MESH)
@@ -114,6 +123,9 @@
                 tok[step, up, half] = token_copy(step, up, half)
     tok[HALF, True, 0] = token_copy(HALF, True, 0)
     tok[HALF, False, 1] = token_copy(HALF, False, 1)
+
+    for load in loads[1:4]:
+        load.wait()
 
     chosen = routes_ref[...]
     erow = iota((EXPERTS, TOK), 0)
@@ -156,6 +168,7 @@
     pl.semaphore_wait(barrier, len(partners))
     for d in (1, 15, 2, 14, 3, 13, 4, 12, 5, 11, 6, 10, 7, 9, 8):
         start(table_copy(d))
+    loads[0].wait()
     for half in range(2):
         for up in (True, False):
             start(tok[1, up, half])
@@ -232,6 +245,17 @@
             many = mm(each, pickone)
             good = (many > slot.astype(F32)) & ((slot >= CAP) if i else (slot < CAP))
             keep[i] = jnp.where(good, 1.0, 0.0).astype(BF16)
+
+    def unfold(part):
+        step = 8
+        count = EXPERTS // step
+
+        def body(i, carry):
+            at = pl.multiple_of(i * step * CAP, step * CAP)
+            inputs_ref[pl.ds(at, step * CAP), :] = inputs_raw[pl.ds(i * step, step)].reshape(step * CAP, HIDDEN)
+            return carry
+
+        lax.fori_loop(part * count, (part + 1) * count, body, 0)
 
     def input_gram(gram, which, i):
         block = 256
@@ -334,26 +358,38 @@
 
     far = remote(mine, theirs, far_sem.at[0], far_sem.at[1], group_dev(4))
 
+    saves = []
+
+    def save(src, dst, at, first):
+        copy = pltpu.make_async_copy(src.at[at], dst.at[at, 0], out_sem.at[first + (1 if at.start else 0)])
+        copy.start()
+        saves.append(copy)
+
     def put_mine(at, value):
         mine[at, :] = value.astype(BF16)
 
     def put_input(at, value):
         input_out[at, :] = (value + theirs[at, :].astype(F32)) * factor
+        save(input_out, input_hbm, at, 0)
 
     def put_grad(at, value):
         grad_out[at, :] = value * factor
-
+        save(grad_out, grad_hbm, at, 2)
+
+    loads[4].wait()
     advance(1, 0)
     send_counts()
     advance(1, 1)
     dispatch(0)
     advance(2, 0)
     masks()
-    input_gram(gram_r, 1, 0)
+    unfold(0)
     advance(2, 1)
     dispatch(1)
+    unfold(1)
+    advance(3, 0)
+    input_gram(gram_r, 1, 0)
     input_gram(gram_r, 1, 1)
-    advance(3, 0)
     input_gram(gram_r, 1, 2)
     rep.first()
     advance(3, 1)
@@ -392,22 +428,34 @@
     gs.last(put_grad)
     for copy in pending:
         copy.wait_send()
+    for copy in saves:
+        copy.wait()
 
 
 def shards(grads, route_weight, routes, hot, expert_inputs):
-    inputs = expert_inputs.reshape(EXPERTS * SLOTS, HIDDEN)
-    vmem = pl.BlockSpec(memory_space=pltpu.VMEM)
+    inputs = expert_inputs.reshape(EXPERTS * 2, CAP, HIDDEN)
+    hbm = pl.BlockSpec(memory_space=pl.ANY)
     dma = pltpu.SemaphoreType.DMA
     hg, hx = WIDTH // NX // 2, HIDDEN // NX // 2
-    grad_rows, input_rows = pl.pallas_call(
+    grad_factor, input_factor = pl.pallas_call(
         kernel,
         out_shape=(
-            jax.ShapeDtypeStruct((WIDTH // NX, WIDTH), F32),
-            jax.ShapeDtypeStruct((HIDDEN // NX, HIDDEN), F32),
+            jax.ShapeDtypeStruct((WIDTH // NX, 1, WIDTH), F32),
+            jax.ShapeDtypeStruct((HIDDEN // NX, 1, HIDDEN), F32),
         ),
-        in_specs=[vmem] * 5,
-        out_specs=(vmem, vmem),
+        in_specs=[hbm] * 5,
+        out_specs=(hbm, hbm),
         scratch_shapes=[
+            pltpu.VMEM((TOP, TOK), jnp.int32),
+            pltpu.VMEM((TOP, TOK), F32),
+            pltpu.VMEM((1, EXPERTS), jnp.int32),
+            pltpu.VMEM((TOK, WIDTH), BF16),
+            pltpu.VMEM((WIDTH // NX, WIDTH), F32),
+            pltpu.VMEM((HIDDEN // NX, HIDDEN), F32),
+            dma((4,)),
+            pltpu.VMEM((EXPERTS * 2, CAP, HIDDEN), BF16),
+            pltpu.VMEM((EXPERTS * SLOTS, HIDDEN), BF16),
+            dma((5,)),
             pltpu.VMEM((HALF, 2 * TOK, WIDTH), BF16),
             pltpu.VMEM((NZ, 1, TOK), F32),
             pltpu.VMEM((NZ, 1, TOK), F32),
@@ -441,10 +489,10 @@
             dma((6,)), dma((6,)), dma((6,)), dma((6,)), dma((6,)), dma((6,)),
         ],
         compiler_params=pltpu.CompilerParams(
-            collective_id=0, has_side_effects=True, vmem_limit_bytes=48 * 1024 * 1024
+            collective_id=0, has_side_effects=True, vmem_limit_bytes=60 * 1024 * 1024
         ),
     )(routes.T, route_weight.T, hot.reshape(1, EXPERTS), grads, inputs)
-    return input_rows[:, None, :], grad_rows[:, None, :]
+    return input_factor, grad_factor
 
 
 def solution(mesh):

time: 98.7 us -> 96.5 us (0.978)
  local copies, waits for them, and re-layouts: 6.27 us -> 3.35 us
    reshape x1 -> x0, local copies, waits for them, and re-layouts: 2.78 us -> none  [shards(): inputs = expert_inputs.reshape(EXPERTS * SLOTS, HIDDEN)]
    unnamed x10 -> x4, local copies, waits for them, and re-layouts: 3.49 us -> 3.35 us
where the time goes in v3:
time: 96.5 us; the launch traced here: 96.3 us
  Pallas kernels  92.3 us (96%)
  local copies, waits for them, and re-layouts  3.35 us (3%)
    pallas_call x1, Pallas kernels, shards(): pl.pallas_call(kernel, out_shape=(jax.ShapeDtypeStruct((WIDTH // NX, 1, W...  92.3 us
    unnamed x4, local copies, waits for them, and re-layouts  3.35 us

profile of v3, /device:TPU:1, one launch (start us, length us, event | category | flops | bytes accessed | tf_op | source)
XLA Modules:
  0.0 96.3 jit_solution(1308949090565829319)
XLA Ops:
  0.6 92.3 %shard_map.68 = (f32[256,1,1024]{2,1,0:T(1,128)}, f32[192,1,768]{2,1,0:T(1,128)}) custom-call(s32[8,128]{1,0:T(8,128)} %bitcast.5, f32[8,128]{1,0:T(8,128)} %bitcast.6, s32[1,128]{1,0:T(1,128)} %bitcast.7, bf16[128,1024]{1,0:T(8,128)(2,1)} %grads_hbm.1, bf16[256,4,768]{2,1,0:T(4,128)(2,1)} %bitcast.4), custom_call_target="tpu_custom_call" | custom-call | tf_op jit(solution)/shard_map/pallas_call | solution.py:440
  93.0 0.0 copy-start
  93.0 2.4 %copy.9 = f32[192,1,768]{2,1,0:T(1,128)} copy(f32[192,1,768]{2,1,0:T(1,128)} %get-tuple-element.8) | data formatting | bytes 1179648
  95.4 0.0 copy-done
  95.4 1.0 %copy.10 = f32[256,1,1024]{2,1,0:T(1,128)} copy(f32[256,1,1024]{2,1,0:T(1,128)S(1)} %copy-done) | data formatting | bytes 2097152
Async XLA Ops:
  93.0 2.4 %copy-start = (f32[256,1,1024]{2,1,0:T(1,128)S(1)}, f32[256,1,1024]{2,1,0:T(1,128)}, u32[]{:S(2)}) copy-start(f32[256,1,1024]{2,1,0:T(1,128)} %get-tuple-element.9) | copy-start | bytes 3145732

commit v4 on v3

--- a/solution.py
+++ b/solution.py
@@ -27,7 +27,7 @@
     routes_hbm, weight_hbm, hot_hbm, grads_hbm, inputs_hbm,
     grad_hbm, input_hbm,
     routes_ref, weight_ref, hot_ref, grads_ref, grad_out, input_out, out_sem, inputs_raw, inputs_ref, in_sem, tokens, table, table_in, keep, counts, counts_in,
-    rows_out, rows_in, gram_g, gram_o, gram_r, mine, theirs,
+    rows_out, rows_in, fold_out, fold_in, fold_send, fold_recv, gram_g, gram_o, gram_r, mine, theirs,
     gs_out, gs_via, gs_l, gs_r, os_out, os_via, os_l, os_r, rs_out, rs_via, rs_l, rs_r,
     tok_send, tok_recv, tab_send, tab_recv, far_sem, cnt_send, cnt_recv,
     row_send, row_recv, gsem_s, gsem_r, osem_s, osem_r, rsem_s, rsem_r,
@@ -190,12 +190,8 @@
     lane = rl.astype(F32)
 
     def dispatch(pair):
-        if pair == HALF - 1:
-            t_l, t_r = table_in[z], table_in[lax.rem(z + HALF, NZ)]
-            g_l = grads_ref[...]
-        else:
-            t_l, t_r = table_in[lax.rem(z + NZ - 1 - pair, NZ)], table_in[lax.rem(z + 1 + pair, NZ)]
-            g_l = tokens[pair, 0:TOK]
+        t_l, t_r = table_in[lax.rem(z + NZ - 1 - pair, NZ)], table_in[lax.rem(z + 1 + pair, NZ)]
+        g_l = tokens[pair, 0:TOK]
         g_r = tokens[pair, TOK:2 * TOK]
         both = jnp.where(from_l, t_l, t_r)
         token_of = jnp.sum(jnp.where(at_token, both, 0.0), axis=1, keepdims=True)
@@ -208,6 +204,36 @@
         for k in (4, 5, 2, 3, 6, 7, 1):
             start(row_copy(pair, k))
         rows_in[pair, 0] = rows_out[pair, j]
+
+    def single_choice(i):
+        t = table_in[lax.rem(z + i * HALF, NZ)]
+        token_of = jnp.sum(jnp.where(at_token, t, 0.0), axis=1, keepdims=True)
+        weight = jnp.sum(jnp.where(at_weight, t, 0.0), axis=1, keepdims=True)
+        return jnp.where(lane == token_of, 1.0, 0.0).astype(BF16), weight
+
+    def dispatch_single(i, hit, weight):
+        half = WIDTH // 2
+        g = tokens[HALF - 1, TOK:2 * TOK] if i else grads_ref[...]
+        found = mm(hit, g)
+        first = lax.rem(iota((GROUP * 2 * SLOTS, half), 0) // SLOTS, 2) == 0
+        rows = (jnp.where(first, found[:, 0:half], found[:, half:WIDTH]) * weight).astype(BF16)
+        fold_out[i] = rows.reshape(GROUP, 2 * SLOTS, half)
+        for k in (4, 5, 2, 3, 6, 7, 1):
+            start(fold_copy(i, k))
+        fold_in[i, 0] = fold_out[i, j]
+
+    def fold_copy(i, k):
+        return remote(fold_out.at[i, group_pos(k)], fold_in.at[i, k],
+                      fold_send.at[i, k], fold_recv.at[i, k], group_dev(k))
+
+    def unfold_rows():
+        whole = []
+        for i in range(2):
+            for k in range(1, GROUP):
+                fold_copy(i, k).wait_recv()
+            f = fold_in[i].astype(F32)
+            whole.append(jnp.concatenate([f[:, 0:SLOTS], f[:, SLOTS:2 * SLOTS]], axis=2))
+        rows_in[HALF - 1] = jnp.concatenate(whole, axis=1).astype(BF16)
 
     def row_copy(pair, k):
         return remote(rows_out.at[pair, group_pos(k)], rows_in.at[pair, k],
@@ -380,6 +406,7 @@
     advance(1, 0)
     send_counts()
     advance(1, 1)
+    dispatch_single(0, *single_choice(0))
     dispatch(0)
     advance(2, 0)
     masks()
@@ -416,14 +443,15 @@
     gram_part(2, 2, False)
     advance(7, 1)
     dispatch(6)
-    gram_part(4, 2, False)
+    last_choice = single_choice(1)
+    advance(8, 0)
+    advance(8, 1)
+    dispatch_single(1, *last_choice)
     far.wait_recv()
     own.last(put_input)
-    advance(8, 0)
-    advance(8, 1)
-    dispatch(7)
-    rows_ready(6, 2)
-    gs.first(lambda blk: gram_rows(6, 2, blk, False))
+    gram_part(4, 3, False)
+    unfold_rows()
+    gs.first(lambda blk: gram_rows(7, 1, blk, False))
     gs.second()
     gs.last(put_grad)
     for copy in pending:
@@ -464,6 +492,9 @@
             pltpu.VMEM((GROUP, NZ, TOK), F32),
             pltpu.VMEM((HALF, GROUP, 2 * SLOTS, WIDTH), BF16),
             pltpu.VMEM((HALF, GROUP, 2 * SLOTS, WIDTH), BF16),
+            pltpu.VMEM((2, GROUP, 2 * SLOTS, WIDTH // 2), BF16),
+            pltpu.VMEM((2, GROUP, 2 * SLOTS, WIDTH // 2), BF16),
+            dma((2, GROUP)), dma((2, GROUP)),
             pltpu.VMEM((WIDTH, WIDTH), F32),
             pltpu.VMEM((HIDDEN, HIDDEN), F32),
             pltpu.VMEM((HIDDEN, HIDDEN), F32),

time: 96.5 us -> 95.9 us (level)
  no operation moved by 1% of the time
where the time goes in v4:
time: 95.9 us; the launch traced here: 95.7 us
  Pallas kernels  91.7 us (96%)
  local copies, waits for them, and re-layouts  3.35 us (3%)
    pallas_call x1, Pallas kernels, shards(): pl.pallas_call(kernel, out_shape=(jax.ShapeDtypeStruct((WIDTH // NX, 1, W...  91.7 us
    unnamed x4, local copies, waits for them, and re-layouts  3.35 us

profile of v4, /device:TPU:1, one launch (start us, length us, event | category | flops | bytes accessed | tf_op | source)
XLA Modules:
  0.0 95.7 jit_solution(9279823373240024994)
XLA Ops:
  0.6 91.7 %shard_map.68 = (f32[256,1,1024]{2,1,0:T(1,128)}, f32[192,1,768]{2,1,0:T(1,128)}) custom-call(s32[8,128]{1,0:T(8,128)} %bitcast.5, f32[8,128]{1,0:T(8,128)} %bitcast.6, s32[1,128]{1,0:T(1,128)} %bitcast.7, bf16[128,1024]{1,0:T(8,128)(2,1)} %grads_hbm.1, bf16[256,4,768]{2,1,0:T(4,128)(2,1)} %bitcast.4), custom_call_target="tpu_custom_call" | custom-call | tf_op jit(solution)/shard_map/pallas_call | solution.py:468
  92.3 0.0 copy-start
  92.4 2.4 %copy.9 = f32[192,1,768]{2,1,0:T(1,128)} copy(f32[192,1,768]{2,1,0:T(1,128)} %get-tuple-element.8) | data formatting | bytes 1179648
  94.7 0.0 copy-done
  94.7 1.0 %copy.10 = f32[256,1,1024]{2,1,0:T(1,128)} copy(f32[256,1,1024]{2,1,0:T(1,128)S(1)} %copy-done) | data formatting | bytes 2097152
Async XLA Ops:
  92.3 2.4 %copy-start = (f32[256,1,1024]{2,1,0:T(1,128)S(1)}, f32[256,1,1024]{2,1,0:T(1,128)}, u32[]{:S(2)}) copy-start(f32[256,1,1024]{2,1,0:T(1,128)} %get-tuple-element.9) | copy-start | bytes 3145732

commit v5 on v4

--- a/solution.py
+++ b/solution.py
@@ -451,10 +451,13 @@
     own.last(put_input)
     gram_part(4, 3, False)
     unfold_rows()
+    before_sum = len(pending)
     gs.first(lambda blk: gram_rows(7, 1, blk, False))
+    for copy in pending[:before_sum]:
+        copy.wait_send()
     gs.second()
     gs.last(put_grad)
-    for copy in pending:
+    for copy in pending[before_sum:]:
         copy.wait_send()
     for copy in saves:
         copy.wait()

time: 95.9 us -> 95.9 us (level)
  no operation moved by 1% of the time
where the time goes in v5:
time: 95.9 us; the launch traced here: 95.7 us
  Pallas kernels  91.7 us (96%)
  local copies, waits for them, and re-layouts  3.35 us (3%)
    pallas_call x1, Pallas kernels, shards(): pl.pallas_call(kernel, out_shape=(jax.ShapeDtypeStruct((WIDTH // NX, 1, W...  91.7 us
    unnamed x4, local copies, waits for them, and re-layouts  3.35 us

profile of v5, /device:TPU:1, one launch (start us, length us, event | category | flops | bytes accessed | tf_op | source)
XLA Modules:
  0.0 95.7 jit_solution(3755455754860546170)
XLA Ops:
  0.6 91.7 %shard_map.68 = (f32[256,1,1024]{2,1,0:T(1,128)}, f32[192,1,768]{2,1,0:T(1,128)}) custom-call(s32[8,128]{1,0:T(8,128)} %bitcast.5, f32[8,128]{1,0:T(8,128)} %bitcast.6, s32[1,128]{1,0:T(1,128)} %bitcast.7, bf16[128,1024]{1,0:T(8,128)(2,1)} %grads_hbm.1, bf16[256,4,768]{2,1,0:T(4,128)(2,1)} %bitcast.4), custom_call_target="tpu_custom_call" | custom-call | tf_op jit(solution)/shard_map/pallas_call | solution.py:471
  92.3 0.0 copy-start
  92.4 2.4 %copy.9 = f32[192,1,768]{2,1,0:T(1,128)} copy(f32[192,1,768]{2,1,0:T(1,128)} %get-tuple-element.8) | data formatting | bytes 1179648
  94.7 0.0 copy-done
  94.7 1.0 %copy.10 = f32[256,1,1024]{2,1,0:T(1,128)} copy(f32[256,1,1024]{2,1,0:T(1,128)S(1)} %copy-done) | data formatting | bytes 2097152
Async XLA Ops:
  92.3 2.4 %copy-start = (f32[256,1,1024]{2,1,0:T(1,128)S(1)}, f32[256,1,1024]{2,1,0:T(1,128)}, u32[]{:S(2)}) copy-start(f32[256,1,1024]{2,1,0:T(1,128)} %get-tuple-element.9) | copy-start | bytes 3145732

commit v6 on v5

--- a/solution.py
+++ b/solution.py
@@ -346,10 +346,14 @@
             lo, hi = pl.ds(0, h), pl.ds(h, h)
             self.c[2].wait_recv()
             self.c[3].wait_recv()
+            low = pl.ds(pl.multiple_of(x * self.rows, 32), h)
+            high = pl.ds(pl.multiple_of(x * self.rows + h, 32), h)
+            self.gram[low, :] += self.r_in[lo].astype(F32)
+            self.gram[high, :] += self.l_in[hi].astype(F32)
             self.c[4].wait_recv()
-            put(lo, self.part(x, 0) + self.l_in[lo].astype(F32) + self.r_in[lo].astype(F32))
+            put(lo, self.part(x, 0) + self.l_in[lo].astype(F32))
             self.c[5].wait_recv()
-            put(hi, self.part(x, 1) + self.l_in[hi].astype(F32) + self.r_in[hi].astype(F32))
+            put(hi, self.part(x, 1) + self.r_in[hi].astype(F32))
 
     factor = 1.0 / (TOK * TOP * NX)
 

time: 95.9 us -> 95.8 us (level)
  no operation moved by 1% of the time
where the time goes in v6:
time: 95.8 us; the launch traced here: 95.6 us
  Pallas kernels  91.6 us (96%)
  local copies, waits for them, and re-layouts  3.35 us (3%)
    pallas_call x1, Pallas kernels, shards(): pl.pallas_call(kernel, out_shape=(jax.ShapeDtypeStruct((WIDTH // NX, 1, W...  91.6 us
    unnamed x4, local copies, waits for them, and re-layouts  3.35 us

profile of v6, /device:TPU:1, one launch (start us, length us, event | category | flops | bytes accessed | tf_op | source)
XLA Modules:
  0.0 95.6 jit_solution(18275058937068882332)
XLA Ops:
  0.6 91.6 %shard_map.68 = (f32[256,1,1024]{2,1,0:T(1,128)}, f32[192,1,768]{2,1,0:T(1,128)}) custom-call(s32[8,128]{1,0:T(8,128)} %bitcast.5, f32[8,128]{1,0:T(8,128)} %bitcast.6, s32[1,128]{1,0:T(1,128)} %bitcast.7, bf16[128,1024]{1,0:T(8,128)(2,1)} %grads_hbm.1, bf16[256,4,768]{2,1,0:T(4,128)(2,1)} %bitcast.4), custom_call_target="tpu_custom_call" | custom-call | tf_op jit(solution)/shard_map/pallas_call | solution.py:475
  92.3 0.0 copy-start
  92.3 2.4 %copy.9 = f32[192,1,768]{2,1,0:T(1,128)} copy(f32[192,1,768]{2,1,0:T(1,128)} %get-tuple-element.8) | data formatting | bytes 1179648
  94.7 0.0 copy-done
  94.7 1.0 %copy.10 = f32[256,1,1024]{2,1,0:T(1,128)} copy(f32[256,1,1024]{2,1,0:T(1,128)S(1)} %copy-done) | data formatting | bytes 2097152
Async XLA Ops:
  92.3 2.4 %copy-start = (f32[256,1,1024]{2,1,0:T(1,128)S(1)}, f32[256,1,1024]{2,1,0:T(1,128)}, u32[]{:S(2)}) copy-start(f32[256,1,1024]{2,1,0:T(1,128)} %get-tuple-element.9) | copy-start | bytes 3145732
